TPU v7x, 512 devices: a whole 4x4x16 slice. The times are simulated.
512 devices in a mesh: turn: 128 (over x_hi, z, y), tm: 4 (over x_lo, core).
Axes of the slice: x: 4 (x_hi: 2, x_lo: 2; x = x_hi * 2 + x_lo), y: 4, z: 16, core: 2. Of those that a mesh axis runs over, the one named last changes fastest.
Arguments:
- voltages: bfloat16 [2048, 32768], P('turn', 'tm'), may hold values from -6 to 6
- gains: float32 [2, 2048, 1024], P(None, None, 'turn'), may hold values from -5 to 5
- dispersion: float32 [1024], P('turn'), may hold values from 50 to 400
Outputs:
- wideband: float32 [1024, 2, 32768], P('turn', None, 'tm')
All inputs are finite; a program needn't handle non-finite values.
Results may differ from a plain program's by a relative error of at most 0.0079.
Values may be sent and summed in bfloat16 or wider, within the bound.
A program may use at most 64 MiB of HBM per device.

v0:
```python
import functools
import math

import jax
import jax.numpy as jnp
import ml_dtypes
import numpy as np
from jax import lax
from jax.experimental import pallas as pl
from jax.experimental.pallas import tpu as pltpu
from jax.sharding import PartitionSpec as P

NFFT = 2048
TAPS = 4
FRAMES = 4
GROUP = 16
QUADS = 8
FEEDS = 256
SHORT = 256
BF16 = jnp.bfloat16
F32 = jnp.float32
MESH = pl.DeviceIdType.MESH
HALF_ROOT = math.sqrt(0.5)


def window_rows():
    extent = TAPS * NFFT
    t = np.arange(extent, dtype=np.float64) + 0.5
    shape = np.sinc((t - 0.5 * extent) / NFFT) * (0.5 - 0.5 * np.cos(t * (2.0 * np.pi / extent)))
    return shape.reshape(TAPS, NFFT).astype(np.float32)


def twiddle_rows():
    angle = 2.0 * np.pi * np.outer(np.arange(8), np.arange(SHORT)) / NFFT
    return (np.stack([np.cos(angle), np.sin(angle)], axis=1) / math.sqrt(NFFT)).astype(np.float32)


def forward_table():
    g, q = np.meshgrid(np.arange(GROUP), np.arange(QUADS), indexing="ij")
    k2 = 16 * q + g
    angle = 2.0 * np.pi * (k2[:, :, None] * np.arange(SHORT) % SHORT) / SHORT
    c, s = np.cos(angle), np.sin(angle)
    real = np.concatenate([c, s], axis=-1)
    imag = np.concatenate([-s, c], axis=-1)
    return np.stack([real, imag], axis=1).reshape(256, 512).astype(ml_dtypes.bfloat16)


def inverse_table():
    g, q = np.meshgrid(np.arange(GROUP), np.arange(QUADS), indexing="ij")
    k2 = (16 * q + g).reshape(-1)
    angle = 2.0 * np.pi * (np.outer(k2, np.arange(SHORT)) % SHORT) / SHORT
    c, s = np.cos(angle), np.sin(angle)
    real = np.concatenate([c, s], axis=1)
    imag = np.concatenate([-s, c], axis=1)
    return np.concatenate([real, imag], axis=0).astype(ml_dtypes.bfloat16)


def beam_table():
    feed = np.arange(FEEDS)
    angle = 2.0 * np.pi * (np.outer(feed, feed) % FEEDS) / FEEDS
    c = np.cos(angle).astype(np.float32).astype(ml_dtypes.bfloat16).astype(np.float32)
    s = np.sin(angle).astype(np.float32).astype(ml_dtypes.bfloat16).astype(np.float32)
    real = np.concatenate([c.T, s.T], axis=1)
    imag = np.concatenate([-s.T, c.T], axis=1)
    both = np.stack([real, imag], axis=1).reshape(32, 4, 2, 2, 512).transpose(1, 0, 2, 3, 4)
    return (both.reshape(512, 512) / 16.0).astype(ml_dtypes.bfloat16)


def spacing_rows():
    g = np.arange(GROUP)[:, None, None, None]
    k1 = np.arange(8)[None, None, :, None]
    q = np.arange(QUADS)[None, None, None, :]
    k = (128 * q + 8 * g + k1 + np.zeros((1, 2, 1, 1), np.int64)).astype(np.float32)
    base = np.float32(1.0) + k / np.float32(1024.0)
    return (np.float32(1.0) / (base * base)).reshape(GROUP, 128).astype(np.float32)


def swap(low, high, axis, by):
    rank = low.ndim
    index = lax.broadcasted_iota(jnp.int32, low.shape, rank - 2 + axis)
    first = (index & by) == 0
    size = low.shape[rank - 2 + axis]
    if axis == 1:
        flat = (-1, low.shape[-1])
        up = pltpu.roll(high.reshape(flat), by, 1).reshape(low.shape)
        down = pltpu.roll(low.reshape(flat), size - by, 1).reshape(low.shape)
    else:
        up = pltpu.roll(high, by, rank - 2)
        down = pltpu.roll(low, size - by, rank - 2)
    return jnp.where(first, low, up), jnp.where(first, down, high)


def exchange(x, bits, lane):
    shape = x.shape
    for b in range(bits):
        split = x.reshape((2 ** (bits - 1 - b), 2, 2**b) + shape[1:])
        low, high = swap(split[:, 0], split[:, 1], 1, lane << b)
        x = jnp.stack([low, high], axis=1).reshape(shape)
    return x


def eight_forward(x):
    s04, d04, s26, d26 = x[0] + x[4], x[0] - x[4], x[2] + x[6], x[2] - x[6]
    s15, d15, s37, d37 = x[1] + x[5], x[1] - x[5], x[3] + x[7], x[3] - x[7]
    even, odd = s04 + s26, s15 + s37
    near, far = HALF_ROOT * (d15 - d37), HALF_ROOT * (d15 + d37)
    y1 = (d04 + near, -(d26 + far))
    y2 = (s04 - s26, s37 - s15)
    y3 = (d04 - near, d26 - far)
    return (even + odd, None), y1, y2, y3, (even - odd, None)


def eight_inverse(a0, a1, a2, a3, a4, b1, b2, b3):
    plus, minus = a0 + a4, a0 - a4
    a13, a31 = a1 + a3, HALF_ROOT * (a1 - a3)
    b13, b31 = HALF_ROOT * (b1 + b3), b1 - b3
    o0, o2 = plus + a2, plus - a2
    m1, m3 = minus - b2, minus + b2
    return (
        o0 + a13, m1 + a31 - b13, o2 - b31, m3 - a31 - b13,
        o0 - a13, m1 - a31 + b13, o2 + b31, m3 + a31 + b13,
    )


def turned_phase(turns):
    return jnp.cos(turns), jnp.sin(turns)


def kernel(
    volt, gain, disp, window, twid, fwd, inv, beam, space, out,
    xv, xh, gv, wv, tv, fv, iv, bv, sv, gb, gr, gt, zs, ab, ra, xs, sb, sr, ct, vs, ys, wf, wb, wr, ov,
    load_sem, out_sem, send_sem, recv_sem,
):
    me, tm = lax.axis_index("turn"), lax.axis_index("tm")
    base, g = (me // GROUP) * GROUP, me % GROUP
    xz, y = me // 4, me % 4
    after, before = (tm + 1) % 4, (tm + 3) % 4

    barrier = pltpu.get_barrier_semaphore()

    def greet_group(i, _):
        pl.semaphore_signal(barrier, inc=1, device_id={"turn": base + (g + i) % GROUP}, device_id_type=MESH)
        return 0

    def greet_quads(i, _):
        pl.semaphore_signal(barrier, inc=1, device_id={"turn": (me + GROUP * i) % 128}, device_id_type=MESH)
        return 0

    for other in (after, before):
        pl.semaphore_signal(barrier, inc=1, device_id={"tm": other}, device_id_type=MESH)
    lax.fori_loop(1, QUADS, greet_quads, 0)
    lax.fori_loop(1, GROUP, greet_group, 0)

    loads = [
        pltpu.make_async_copy(a, b, load_sem.at[i])
        for i, (a, b) in enumerate(
            [(volt, xv), (gain, gv), (window, wv), (twid, tv), (fwd, fv), (inv, iv), (beam, bv), (space, sv)]
        )
    ]
    for load in loads:
        load.start()
    loads[0].wait()
    loads[1].wait()
    gb[...] = gv[...].reshape(16, 2048).astype(BF16)
    pl.semaphore_wait(barrier, 2 + QUADS - 1 + GROUP - 1)

    history = pltpu.make_async_remote_copy(
        src_ref=xv.at[:, pl.ds(NFFT, 3 * NFFT)], dst_ref=xh, send_sem=send_sem.at[0], recv_sem=recv_sem.at[0],
        device_id={"tm": after}, device_id_type=MESH,
    )
    history.start()

    mine = me // GROUP

    def send_gain(i, _):
        q = (mine + i) % QUADS
        pltpu.make_async_remote_copy(
            src_ref=gb.at[:, pl.ds(pl.multiple_of(q * FEEDS, FEEDS), FEEDS)], dst_ref=gr.at[mine],
            send_sem=send_sem.at[1], recv_sem=recv_sem.at[1],
            device_id={"turn": q * GROUP + g}, device_id_type=MESH,
        ).start()
        return 0

    lax.fori_loop(1, QUADS, send_gain, 0)
    gr[mine] = gb[:, pl.ds(pl.multiple_of(mine * FEEDS, FEEDS), FEEDS)]

    for i in (2, 3, 4):
        loads[i].wait()
    keep = jnp.where(tm > 0, 1.0, 0.0).astype(F32)

    def frame_of(at):
        if at < 0:
            return xh[:, pl.ds((at + 3) * NFFT, NFFT)].astype(F32) * keep
        return xv[:, pl.ds(at * NFFT, NFFT)].astype(F32)

    def channelize(f):
        total = wv[0:1, :] * frame_of(f - 3)
        for p in range(1, TAPS):
            total = total + wv[p : p + 1, :] * frame_of(f - 3 + p)
        total = total.astype(BF16).astype(F32)
        parts = eight_forward([total[:, n * SHORT : (n + 1) * SHORT] for n in range(8)])
        for k1 in range(8):
            re, im = parts[k1] if k1 < 5 else parts[8 - k1]
            c, s = tv[k1, 0:1, :], -tv[k1, 1:2, :]
            if im is None:
                zr, zi = re * c, re * s
            elif k1 < 5:
                zr, zi = re * c - im * s, re * s + im * c
            else:
                zr, zi = re * c + im * s, re * s - im * c
            rows = pl.ds((f * 8 + k1) * 16, 16)
            zs[rows, 0:SHORT] = zr.astype(BF16)
            zs[rows, SHORT : 2 * SHORT] = zi.astype(BF16)

    channelize(3)
    history.wait_recv()
    for f in range(3):
        channelize(f)
    contract = (((1,), (1,)), ((), ()))
    ab[...] = lax.dot_general(fv[...], zs[...], contract, preferred_element_type=F32).astype(BF16)

    def send_channels(i, _):
        to = (g + i) % GROUP
        pltpu.make_async_remote_copy(
            src_ref=ab.at[pl.ds(pl.multiple_of(to * 16, 16), 16), :], dst_ref=ra.at[g],
            send_sem=send_sem.at[2], recv_sem=recv_sem.at[2],
            device_id={"turn": base + to}, device_id_type=MESH,
        ).start()
        return 0

    lax.fori_loop(1, GROUP, send_channels, 0)
    ra[g] = ab[pl.ds(pl.multiple_of(g * 16, 16), 16), :]

    pltpu.make_async_copy(gr.at[pl.ds(0, QUADS - 1)], gr.at[pl.ds(0, QUADS - 1)], recv_sem.at[1]).wait()
    for half in range(2):
        got = gr[:, :, half * 128 : (half + 1) * 128].astype(F32).reshape(QUADS, 2, 8, 128)
        for b in range(3):
            split = got.reshape(2 ** (2 - b), 2, 2**b, 2, 8, 128)
            flat = (-1, 8, 128)
            low, high = swap(split[:, 0].reshape(flat), split[:, 1].reshape(flat), 0, 1 << b)
            part = (2 ** (2 - b), 2**b, 2, 8, 128)
            got = jnp.stack([low.reshape(part), high.reshape(part)], axis=1).reshape(QUADS, 2, 8, 128)
        gt[half] = got

    loads[7].wait()
    row = lax.broadcasted_iota(jnp.int32, (8, 128), 0)

    def phases(at, _):
        for e in range(4):
            scale = jnp.where((row & 2) == 0, disp[e], disp[4 + e])
            c, s = turned_phase(scale * sv[pl.ds(at, 1), :])
            ct[at, 0, e] = 0.5 * c
            ct[at, 1, e] = 0.5 * s
        return 0

    lax.fori_loop(0, GROUP, phases, 0)

    loads[6].wait()
    loads[5].wait()
    pltpu.make_async_copy(ra.at[pl.ds(0, GROUP - 1)], ra.at[pl.ds(0, GROUP - 1)], recv_sem.at[2]).wait()

    for f in range(FRAMES):
        for half in range(2):
            got = ra[half * 8 : (half + 1) * 8, :, f * 128 : (f + 1) * 128].astype(F32)
            got = exchange(got.reshape(8, 2, 8, 128), 3, 16)
            re, im = got[:, 0], got[:, 1]
            gre, gim = gt[half, :, 0], gt[half, :, 1]
            rows = pl.ds(f * 64, 64)
            xs[rows, half * 128 : (half + 1) * 128] = (gre * re - gim * im).reshape(64, 128).astype(BF16)
            xs[rows, FEEDS + half * 128 : FEEDS + (half + 1) * 128] = (gre * im + gim * re).reshape(64, 128).astype(BF16)

    row3 = lax.broadcasted_iota(jnp.int32, (16, 8, 128), 1)
    for c in range(4):
        to_y = (y + c) % 4
        both = lax.dot_general(
            bv[pl.ds(pl.multiple_of(to_y * 128, 128), 128), :], xs[...], contract, preferred_element_type=F32
        )
        low, high = both[:, :128].reshape(16, 8, 128), both[:, 128:].reshape(16, 8, 128)
        sb[to_y, :, 0] = jnp.where(row3 < 4, low, pltpu.roll(high, 4, 1)).astype(BF16)
        sb[to_y, :, 1] = jnp.where(row3 < 4, pltpu.roll(low, 4, 1), high).astype(BF16)

        def send_beams(i, _):
            to = (xz + i) % 32
            pltpu.make_async_remote_copy(
                src_ref=sb.at[to_y, to // 2, to % 2], dst_ref=sr.at[me],
                send_sem=send_sem.at[3], recv_sem=recv_sem.at[3],
                device_id={"turn": to * 4 + to_y}, device_id_type=MESH,
            ).start()
            return 0

        lax.fori_loop(1 if c == 0 else 0, 32, send_beams, 0)
    sr[me] = sb[y, xz // 2, xz % 2]

    pltpu.make_async_copy(sr.at[pl.ds(0, 127)], sr.at[pl.ds(0, 127)], recv_sem.at[3]).wait()

    def east_west(at, _):
        ns = [[None] * 4, [None] * 4]
        for c in range(4):
            one = sr[c * GROUP + at].astype(F32)
            two = sr[64 + c * GROUP + at].astype(F32)
            ns[0][c], ns[1][c] = swap(one, two, 0, 1)
        (r0, r1, r2, r3), (i0, i1, i2, i3) = ns
        ra_, rb_, rc_, rd_ = r0 + r2, r0 - r2, r1 + r3, r1 - r3
        ia_, ib_, ic_, id_ = i0 + i2, i0 - i2, i1 + i3, i1 - i3
        beams = [(ra_ + rc_, ia_ + ic_), (rb_ + id_, ib_ - rd_), (ra_ - rc_, ia_ - ic_), (rb_ - id_, ib_ + rd_)]
        chirped = []
        for e in range(4):
            re, im = beams[e]
            c, s = ct[at, 0, e], ct[at, 1, e]
            chirped.append((re * c - im * s, re * s + im * c))
        for high in range(2):
            for r in range(2):
                first, second = swap(chirped[2 * high][r], chirped[2 * high + 1][r], 0, 4)
                vs[r, 0, at, high] = first
                vs[r, 1, at, high] = second
        return 0

    lax.fori_loop(0, GROUP, east_west, 0)

    for r in range(2):
        for h in range(2):
            turned = exchange(vs[r, h], 4, 8).reshape(2, 8, 16, 128).astype(BF16)
            ys[2 * h, :, :, r * 128 : (r + 1) * 128] = turned[0]
            ys[2 * h + 1, :, :, r * 128 : (r + 1) * 128] = turned[1]

    def synthesise(f):
        z = jnp.dot(ys[f].reshape(128, 256), iv[...], preferred_element_type=F32).reshape(8, 16, 512)
        re, im = [], []
        for k1 in range(8):
            zr, zi = z[k1, :, :SHORT], z[k1, :, SHORT:]
            c, s = tv[k1, 0:1, :], tv[k1, 1:2, :]
            re.append(zr * c - zi * s)
            im.append(zr * s + zi * c if k1 % 4 else None)
        outs = eight_inverse(
            re[0], re[1] + re[7], re[2] + re[6], re[3] + re[5], re[4],
            im[1] - im[7], im[2] - im[6], im[3] - im[5],
        )
        for n in range(8):
            wf[f, :, n * SHORT : (n + 1) * SHORT] = outs[n]
            if f < 3:
                wb[f, :, n * SHORT : (n + 1) * SHORT] = outs[n].astype(BF16)

    for f in range(3):
        synthesise(f)
    future = pltpu.make_async_remote_copy(
        src_ref=wb, dst_ref=wr, send_sem=send_sem.at[4], recv_sem=recv_sem.at[4],
        device_id={"tm": before}, device_id_type=MESH,
    )
    future.start()
    synthesise(3)

    last = jnp.where(tm < 3, 1.0, 0.0).astype(F32)

    def wave_of(at):
        if at > 3:
            return wr[at - 4].astype(F32) * last
        return wf[at]

    stores = []
    for f in range(FRAMES):
        if f == 1:
            future.wait_recv()
        total = wv[3:4, :] * wave_of(f)
        for p in range(1, TAPS):
            total = total + wv[3 - p : 4 - p, :] * wave_of(f + p)
        ov[:, f * NFFT : (f + 1) * NFFT] = total
        store = pltpu.make_async_copy(
            ov.at[:, pl.ds(f * NFFT, NFFT)], out.at[:, pl.ds(f * NFFT, NFFT)], out_sem.at[f]
        )
        store.start()
        stores.append(store)

    history.wait_send()
    future.wait_send()
    pltpu.make_async_copy(gr.at[pl.ds(0, QUADS - 1)], gr.at[pl.ds(0, QUADS - 1)], send_sem.at[1]).wait()
    pltpu.make_async_copy(ra.at[pl.ds(0, GROUP - 1)], ra.at[pl.ds(0, GROUP - 1)], send_sem.at[2]).wait()
    pltpu.make_async_copy(sr.at[pl.ds(0, 127)], sr.at[pl.ds(0, 127)], send_sem.at[3]).wait()
    for store in stores:
        store.wait()


def body(voltages, gains, dispersion):
    anywhere = pl.BlockSpec(memory_space=pl.ANY)
    vmem = pltpu.VMEM
    rows = pl.pallas_call(
        kernel,
        out_shape=jax.ShapeDtypeStruct((16, FRAMES * NFFT), F32),
        in_specs=[anywhere, anywhere, pl.BlockSpec(memory_space=pltpu.SMEM)] + [anywhere] * 6,
        out_specs=anywhere,
        scratch_shapes=[
            vmem((16, FRAMES * NFFT), BF16),
            vmem((16, 3 * NFFT), BF16),
            vmem((2, 8, 2048), F32),
            vmem((TAPS, NFFT), F32),
            vmem((8, 2, SHORT), F32),
            vmem((256, 512), BF16),
            vmem((256, 512), BF16),
            vmem((512, 512), BF16),
            vmem((GROUP, 128), F32),
            vmem((16, 2048), BF16),
            vmem((QUADS, 16, FEEDS), BF16),
            vmem((2, 8, 2, 8, 128), F32),
            vmem((512, 512), BF16),
            vmem((256, 512), BF16),
            vmem((GROUP, 16, 512), BF16),
            vmem((256, 512), BF16),
            vmem((4, 16, 2, 8, 128), BF16),
            vmem((128, 8, 128), BF16),
            vmem((GROUP, 2, 4, 8, 128), F32),
            vmem((2, 2, GROUP, 2, 8, 128), F32),
            vmem((FRAMES, 8, 16, 256), BF16),
            vmem((FRAMES, 16, NFFT), F32),
            vmem((3, 16, NFFT), BF16),
            vmem((3, 16, NFFT), BF16),
            vmem((16, FRAMES * NFFT), F32),
            pltpu.SemaphoreType.DMA((8,)),
            pltpu.SemaphoreType.DMA((FRAMES,)),
            pltpu.SemaphoreType.DMA((5,)),
            pltpu.SemaphoreType.DMA((5,)),
        ],
        compiler_params=pltpu.CompilerParams(
            collective_id=0, has_side_effects=True, vmem_limit_bytes=40 * 1024 * 1024
        ),
        cost_estimate=pl.CostEstimate(flops=500_000_000, bytes_accessed=3_000_000, transcendentals=0),
    )(
        voltages, gains.transpose(0, 2, 1), dispersion,
        window_rows(), twiddle_rows(), forward_table(), inverse_table(), beam_table(), spacing_rows(),
    )
    ordered = rows.reshape(4, 2, 2, FRAMES * NFFT).transpose(1, 0, 2, 3)
    return ordered.reshape(8, 2, FRAMES * NFFT)


def solution(mesh):
    placed = (P("turn", "tm"), P(None, None, "turn"), P("turn"))
    return jax.shard_map(
        body, mesh=mesh, in_specs=placed, out_specs=P("turn", None, "tm"), check_vma=False
    )
```

profile of v0, /device:TPU:1, one launch (start us, length us, event | category | flops | bytes accessed | tf_op | source)
XLA Modules:
  0.0 61.0 jit_solution(1637156199953562972)
XLA Ops:
  0.0 0.0 copy-start.7
  0.0 0.0 copy-start.8
  0.0 0.7 %copy-done.7 = f32[16,128]{1,0:T(8,128)S(1)} copy-done((f32[16,128]{1,0:T(8,128)S(1)}, f32[16,128]{1,0:T(8,128)}, u32[]{:S(2)}) %copy-start.7) | copy-done | bytes 8216
  0.7 0.0 copy-done.8
  0.7 0.0 copy-start
  0.7 1.0 %copy-done = bf16[512,512]{1,0:T(8,128)(2,1)S(1)} copy-done((bf16[512,512]{1,0:T(8,128)(2,1)S(1)}, bf16[512,512]{1,0:T(8,128)(2,1)}, u32[]{:S(2)}) %copy-start) | copy-done | bytes 524312
  1.7 0.0 copy-start.1
  1.7 0.9 %copy-done.1 = bf16[16,8192]{1,0:T(8,128)(2,1)S(1)} copy-done((bf16[16,8192]{1,0:T(8,128)(2,1)S(1)}, bf16[16,8192]{1,0:T(8,128)(2,1)}, u32[]{:S(2)}) %copy-start.1) | copy-done | bytes 262168
  2.7 0.0 copy-start.2
  2.7 0.9 %copy-done.2 = bf16[256,512]{1,0:T(8,128)(2,1)S(1)} copy-done((bf16[256,512]{1,0:T(8,128)(2,1)S(1)}, bf16[256,512]{1,0:T(8,128)(2,1)}, u32[]{:S(2)}) %copy-start.2) | copy-done | bytes 262168
  3.6 0.0 copy-start.3
  3.6 0.9 %copy-done.3 = bf16[256,512]{1,0:T(8,128)(2,1)S(1)} copy-done((bf16[256,512]{1,0:T(8,128)(2,1)S(1)}, bf16[256,512]{1,0:T(8,128)(2,1)}, u32[]{:S(2)}) %copy-start.3) | copy-done | bytes 262168
  4.6 0.0 copy-start.4
  4.6 0.9 %copy-done.4 = f32[2,2048,8]{1,2,0:T(8,128)S(1)} copy-done((f32[2,2048,8]{1,2,0:T(8,128)S(1)}, f32[2,2048,8]{1,2,0:T(8,128)}, u32[]{:S(2)}) %copy-start.4) | copy-done | bytes 131096
  5.5 0.0 copy-start.5
  5.5 0.8 %copy-done.5 = f32[4,2048]{1,0:T(4,128)S(1)} copy-done((f32[4,2048]{1,0:T(4,128)S(1)}, f32[4,2048]{1,0:T(4,128)}, u32[]{:S(2)}) %copy-start.5) | copy-done | bytes 32792
  6.3 0.0 copy-start.6
  6.3 0.7 %copy-done.6 = f32[8,2,256]{2,1,0:T(2,128)S(1)} copy-done((f32[8,2,256]{2,1,0:T(2,128)S(1)}, f32[8,2,256]{2,1,0:T(2,128)}, u32[]{:S(2)}) %copy-start.6) | copy-done | bytes 16408
  7.0 52.9 %shard_map.91 = f32[16,8192]{1,0:T(8,128)S(1)} custom-call(bf16[16,8192]{1,0:T(8,128)(2,1)S(1)} %copy-done.1, f32[2,8,2048]{2,1,0:T(8,128)S(1)} %bitcast.3, f32[8]{0:T(128)S(1)} %copy-done.8, f32[4,2048]{1,0:T(4,128)S(1)} %copy-done.5, f32[8,2,256]{2,1,0:T(2,128)S(1)} %copy-done.6, bf16[256,512]{1,0:T(8,128)(2,1)S(1)} %copy-done.3, ...), custom_call_target="tpu_custom_call" | custom-call | flops 500000000 | bytes 3000000 | tf_op jit(solution)/shard_map/pallas_call | solution.py:385
  59.9 0.3 reshape.6
  60.2 0.8 %copy.10 = f32[2,4,2,8192]{3,2,1,0:T(2,128)} copy(f32[2,4,2,8192]{3,2,0,1:T(2,128)S(1)} %bitcast.4) | data formatting | bytes 1048576 | tf_op jit(solution)/shard_map/transpose | solution.py:429
Async XLA Ops:
  0.0 0.7 %copy-start.7 = (f32[16,128]{1,0:T(8,128)S(1)}, f32[16,128]{1,0:T(8,128)}, u32[]{:S(2)}) copy-start(f32[16,128]{1,0:T(8,128)} %constant.17.clone.space) | copy-start | bytes 24580
  0.0 0.7 %copy-start.8 = (f32[8]{0:T(128)S(1)}, f32[8]{0:T(128)}, u32[]{:S(2)}) copy-start(f32[8]{0:T(128)} %disp.1) | copy-start | bytes 100
  0.7 1.0 %copy-start = (bf16[512,512]{1,0:T(8,128)(2,1)S(1)}, bf16[512,512]{1,0:T(8,128)(2,1)}, u32[]{:S(2)}) copy-start(bf16[512,512]{1,0:T(8,128)(2,1)} %constant.16.clone.beam) | copy-start | bytes 1572868
  1.7 0.9 %copy-start.1 = (bf16[16,8192]{1,0:T(8,128)(2,1)S(1)}, bf16[16,8192]{1,0:T(8,128)(2,1)}, u32[]{:S(2)}) copy-start(bf16[16,8192]{1,0:T(8,128)(2,1)} %volt.1) | copy-start | bytes 786436
  2.7 0.9 %copy-start.2 = (bf16[256,512]{1,0:T(8,128)(2,1)S(1)}, bf16[256,512]{1,0:T(8,128)(2,1)}, u32[]{:S(2)}) copy-start(bf16[256,512]{1,0:T(8,128)(2,1)} %constant.15.clone.inv) | copy-start | bytes 786436
  3.6 0.9 %copy-start.3 = (bf16[256,512]{1,0:T(8,128)(2,1)S(1)}, bf16[256,512]{1,0:T(8,128)(2,1)}, u32[]{:S(2)}) copy-start(bf16[256,512]{1,0:T(8,128)(2,1)} %constant.14.clone.fwd) | copy-start | bytes 786436
  4.6 0.9 %copy-start.4 = (f32[2,2048,8]{1,2,0:T(8,128)S(1)}, f32[2,2048,8]{1,2,0:T(8,128)}, u32[]{:S(2)}) copy-start(f32[2,2048,8]{1,2,0:T(8,128)} %param.10) | copy-start | bytes 393220
  5.5 0.8 %copy-start.5 = (f32[4,2048]{1,0:T(4,128)S(1)}, f32[4,2048]{1,0:T(4,128)}, u32[]{:S(2)}) copy-start(f32[4,2048]{1,0:T(4,128)} %constant.12.clone.window) | copy-start | bytes 98308
  6.3 0.7 %copy-start.6 = (f32[8,2,256]{2,1,0:T(2,128)S(1)}, f32[8,2,256]{2,1,0:T(2,128)}, u32[]{:S(2)}) copy-start(f32[8,2,256]{2,1,0:T(2,128)} %constant.13.clone.twid) | copy-start | bytes 49156
where the time goes:
time: 61.4 us; the launch traced here: 61 us
  Pallas kernels  52.9 us (86%)
  local copies, waits for them, and re-layouts  8.1 us (13%)
    pallas_call x1, Pallas kernels, body(): pl.pallas_call(kernel, out_shape=jax.ShapeDtypeStruct((16, FRAMES * NFFT)...  52.9 us
    unnamed x18, local copies, waits for them, and re-layouts  6.97 us

commit v1 on v0

--- a/solution.py
+++ b/solution.py
@@ -72,7 +72,8 @@
     q = np.arange(QUADS)[None, None, None, :]
     k = (128 * q + 8 * g + k1 + np.zeros((1, 2, 1, 1), np.int64)).astype(np.float32)
     base = np.float32(1.0) + k / np.float32(1024.0)
-    return (np.float32(1.0) / (base * base)).reshape(GROUP, 128).astype(np.float32)
+    rows = (np.float32(1.0) / (base * base)).reshape(GROUP, 128).astype(np.float32)
+    return np.stack([np.roll(rows[i], 8 * i) for i in range(GROUP)])
 
 
 def swap(low, high, axis, by):
@@ -90,13 +91,15 @@
     return jnp.where(first, low, up), jnp.where(first, down, high)
 
 
-def exchange(x, bits, lane):
-    shape = x.shape
-    for b in range(bits):
-        split = x.reshape((2 ** (bits - 1 - b), 2, 2**b) + shape[1:])
-        low, high = swap(split[:, 0], split[:, 1], 1, lane << b)
-        x = jnp.stack([low, high], axis=1).reshape(shape)
-    return x
+def gather(parts, lane):
+    n = len(parts)
+    index = lax.broadcasted_iota(jnp.int32, parts[0].shape, 1)
+    by = 1
+    while by < n:
+        here = (index & (by * lane)) == 0
+        parts = [jnp.where(here, parts[i], parts[(i + by) % n]) for i in range(n)]
+        by *= 2
+    return [pltpu.roll(parts[(n - k) % n], (n - k) * lane, 1) if k else parts[0] for k in range(n)]
 
 
 def eight_forward(x):
@@ -128,8 +131,8 @@
 
 def kernel(
     volt, gain, disp, window, twid, fwd, inv, beam, space, out,
-    xv, xh, gv, wv, tv, fv, iv, bv, sv, gb, gr, gt, zs, ab, ra, xs, sb, sr, ct, vs, ys, wf, wb, wr, ov,
-    load_sem, out_sem, send_sem, recv_sem,
+    xv, xh, gv, wv, tv, fv, iv, bv, sv, gb, gr, gt, zs, ab, ra, xs, xb, sb, sr, ct, vs, ys, wf, wb, wr, ov,
+    load_sem, out_sem, send_sem, recv_sem, hist_sem, chan_sem, beam_sem, fut_sem,
 ):
     me, tm = lax.axis_index("turn"), lax.axis_index("tm")
     base, g = (me // GROUP) * GROUP, me % GROUP
@@ -164,25 +167,16 @@
     gb[...] = gv[...].reshape(16, 2048).astype(BF16)
     pl.semaphore_wait(barrier, 2 + QUADS - 1 + GROUP - 1)
 
-    history = pltpu.make_async_remote_copy(
-        src_ref=xv.at[:, pl.ds(NFFT, 3 * NFFT)], dst_ref=xh, send_sem=send_sem.at[0], recv_sem=recv_sem.at[0],
-        device_id={"tm": after}, device_id_type=MESH,
-    )
-    history.start()
-
-    mine = me // GROUP
-
-    def send_gain(i, _):
-        q = (mine + i) % QUADS
+    history = [
         pltpu.make_async_remote_copy(
-            src_ref=gb.at[:, pl.ds(pl.multiple_of(q * FEEDS, FEEDS), FEEDS)], dst_ref=gr.at[mine],
-            send_sem=send_sem.at[1], recv_sem=recv_sem.at[1],
-            device_id={"turn": q * GROUP + g}, device_id_type=MESH,
-        ).start()
-        return 0
-
-    lax.fori_loop(1, QUADS, send_gain, 0)
-    gr[mine] = gb[:, pl.ds(pl.multiple_of(mine * FEEDS, FEEDS), FEEDS)]
+            src_ref=xv.at[:, pl.ds((slot + 1) * NFFT, NFFT)], dst_ref=xh.at[slot],
+            send_sem=hist_sem.at[0, slot], recv_sem=hist_sem.at[1, slot],
+            device_id={"tm": after}, device_id_type=MESH,
+        )
+        for slot in range(3)
+    ]
+    for slot in (2, 1, 0):
+        history[slot].start()
 
     for i in (2, 3, 4):
         loads[i].wait()
@@ -190,7 +184,7 @@
 
     def frame_of(at):
         if at < 0:
-            return xh[:, pl.ds((at + 3) * NFFT, NFFT)].astype(F32) * keep
+            return xh[at + 3].astype(F32) * keep
         return xv[:, pl.ds(at * NFFT, NFFT)].astype(F32)
 
     def channelize(f):
@@ -208,30 +202,51 @@
                 zr, zi = re * c - im * s, re * s + im * c
             else:
                 zr, zi = re * c + im * s, re * s - im * c
-            rows = pl.ds((f * 8 + k1) * 16, 16)
-            zs[rows, 0:SHORT] = zr.astype(BF16)
-            zs[rows, SHORT : 2 * SHORT] = zi.astype(BF16)
+            rows = pl.ds(pl.multiple_of((k1 + g) % 8 * 16, 16), 16)
+            zs[f, rows, 0:SHORT] = zr.astype(BF16)
+            zs[f, rows, SHORT : 2 * SHORT] = zi.astype(BF16)
+
+    contract = (((1,), (1,)), ((), ()))
+
+    def exchange_channels(f):
+        channels = lax.dot_general(fv[...], zs[f], contract, preferred_element_type=F32)
+        ab[f] = channels.reshape(GROUP, 16, 128).astype(BF16)
+
+        def send_channels(i, _):
+            to = (g + i) % GROUP
+            pltpu.make_async_remote_copy(
+                src_ref=ab.at[f, to], dst_ref=ra.at[f, g],
+                send_sem=send_sem.at[1], recv_sem=chan_sem.at[f],
+                device_id={"turn": base + to}, device_id_type=MESH,
+            ).start()
+            return 0
+
+        lax.fori_loop(1, GROUP, send_channels, 0)
+        ra[f, g] = ab[f, g]
 
     channelize(3)
-    history.wait_recv()
-    for f in range(3):
-        channelize(f)
-    contract = (((1,), (1,)), ((), ()))
-    ab[...] = lax.dot_general(fv[...], zs[...], contract, preferred_element_type=F32).astype(BF16)
-
-    def send_channels(i, _):
-        to = (g + i) % GROUP
+    exchange_channels(3)
+
+    mine = me // GROUP
+
+    def send_gain(i, _):
+        q = (mine + i) % QUADS
         pltpu.make_async_remote_copy(
-            src_ref=ab.at[pl.ds(pl.multiple_of(to * 16, 16), 16), :], dst_ref=ra.at[g],
-            send_sem=send_sem.at[2], recv_sem=recv_sem.at[2],
-            device_id={"turn": base + to}, device_id_type=MESH,
+            src_ref=gb.at[:, pl.ds(pl.multiple_of(q * FEEDS, FEEDS), FEEDS)], dst_ref=gr.at[mine],
+            send_sem=send_sem.at[0], recv_sem=recv_sem.at[0],
+            device_id={"turn": q * GROUP + g}, device_id_type=MESH,
         ).start()
         return 0
 
-    lax.fori_loop(1, GROUP, send_channels, 0)
-    ra[g] = ab[pl.ds(pl.multiple_of(g * 16, 16), 16), :]
-
-    pltpu.make_async_copy(gr.at[pl.ds(0, QUADS - 1)], gr.at[pl.ds(0, QUADS - 1)], recv_sem.at[1]).wait()
+    lax.fori_loop(1, QUADS, send_gain, 0)
+    gr[mine] = gb[:, pl.ds(pl.multiple_of(mine * FEEDS, FEEDS), FEEDS)]
+
+    for f in (2, 1, 0):
+        history[f].wait_recv()
+        channelize(f)
+        exchange_channels(f)
+
+    pltpu.make_async_copy(gr.at[pl.ds(0, QUADS - 1)], gr.at[pl.ds(0, QUADS - 1)], recv_sem.at[0]).wait()
     for half in range(2):
         got = gr[:, :, half * 128 : (half + 1) * 128].astype(F32).reshape(QUADS, 2, 8, 128)
         for b in range(3):
@@ -242,6 +257,55 @@
             got = jnp.stack([low.reshape(part), high.reshape(part)], axis=1).reshape(QUADS, 2, 8, 128)
         gt[half] = got
 
+    loads[6].wait()
+    loads[5].wait()
+    for f in (3, 2, 1, 0):
+        pltpu.make_async_copy(ra.at[f, pl.ds(0, GROUP - 1)], ra.at[f, pl.ds(0, GROUP - 1)], chan_sem.at[f]).wait()
+        for half in range(2):
+            items = gather([ra[f, half * 8 + i].astype(F32) for i in range(8)], 16)
+            for k1 in range(8):
+                re, im = items[k1][:8], items[k1][8:]
+                gre, gim = gt[half, k1, 0], gt[half, k1, 1]
+                rows = pl.ds(pl.multiple_of((f // 2) * 128 + ((f % 2) * 8 + k1 + g) % 16 * 8, 8), 8)
+                xs[rows, half * 128 : (half + 1) * 128] = gre * re - gim * im
+                xs[rows, FEEDS + half * 128 : FEEDS + (half + 1) * 128] = gre * im + gim * re
+    xb[...] = xs[...].astype(BF16)
+
+    row3 = lax.broadcasted_iota(jnp.int32, (16, 8, 128), 1)
+    xh_me, z_me = me // 64, xz % 16
+    for pair in range(2):
+        for c in (2 * pair, 2 * pair + 1):
+            to_y = (y + c) % 4
+            both = lax.dot_general(
+                bv[pl.ds(pl.multiple_of(to_y * 128, 128), 128), :], xb[...], contract, preferred_element_type=F32
+            )
+            low, high = both[:, :128].reshape(16, 8, 128), both[:, 128:].reshape(16, 8, 128)
+            sb[to_y, :, 0] = jnp.where(row3 < 4, low, pltpu.roll(high, 4, 1)).astype(BF16)
+            sb[to_y, :, 1] = jnp.where(row3 < 4, pltpu.roll(low, 4, 1), high).astype(BF16)
+
+        def send_beams(c, x_by, z_by):
+            to_y = (y + c) % 4
+            to = ((xh_me + x_by) % 2) * 16 + (z_me + z_by) % 16
+            pltpu.make_async_remote_copy(
+                src_ref=sb.at[to_y, to // 2, to % 2], dst_ref=sr.at[me],
+                send_sem=send_sem.at[2], recv_sem=beam_sem.at[c],
+                device_id={"turn": to * 4 + to_y}, device_id_type=MESH,
+            ).start()
+
+        def send_far(i, _):
+            z_by = 8 + (1 - 2 * (i % 2)) * ((i + 1) // 2)
+            for c in (2 * pair, 2 * pair + 1):
+                for x_by in range(2):
+                    send_beams(c, x_by, z_by)
+            return 0
+
+        lax.fori_loop(0, 15, send_far, 0)
+        for c in (2 * pair, 2 * pair + 1):
+            for x_by in range(2):
+                if c + x_by > 0:
+                    send_beams(c, x_by, 0)
+    sr[me] = sb[y, xz // 2, xz % 2]
+
     loads[7].wait()
     row = lax.broadcasted_iota(jnp.int32, (8, 128), 0)
 
@@ -255,45 +319,8 @@
 
     lax.fori_loop(0, GROUP, phases, 0)
 
-    loads[6].wait()
-    loads[5].wait()
-    pltpu.make_async_copy(ra.at[pl.ds(0, GROUP - 1)], ra.at[pl.ds(0, GROUP - 1)], recv_sem.at[2]).wait()
-
-    for f in range(FRAMES):
-        for half in range(2):
-            got = ra[half * 8 : (half + 1) * 8, :, f * 128 : (f + 1) * 128].astype(F32)
-            got = exchange(got.reshape(8, 2, 8, 128), 3, 16)
-            re, im = got[:, 0], got[:, 1]
-            gre, gim = gt[half, :, 0], gt[half, :, 1]
-            rows = pl.ds(f * 64, 64)
-            xs[rows, half * 128 : (half + 1) * 128] = (gre * re - gim * im).reshape(64, 128).astype(BF16)
-            xs[rows, FEEDS + half * 128 : FEEDS + (half + 1) * 128] = (gre * im + gim * re).reshape(64, 128).astype(BF16)
-
-    row3 = lax.broadcasted_iota(jnp.int32, (16, 8, 128), 1)
-    for c in range(4):
-        to_y = (y + c) % 4
-        both = lax.dot_general(
-            bv[pl.ds(pl.multiple_of(to_y * 128, 128), 128), :], xs[...], contract, preferred_element_type=F32
-        )
-        low, high = both[:, :128].reshape(16, 8, 128), both[:, 128:].reshape(16, 8, 128)
-        sb[to_y, :, 0] = jnp.where(row3 < 4, low, pltpu.roll(high, 4, 1)).astype(BF16)
-        sb[to_y, :, 1] = jnp.where(row3 < 4, pltpu.roll(low, 4, 1), high).astype(BF16)
-
-        def send_beams(i, _):
-            to = (xz + i) % 32
-            pltpu.make_async_remote_copy(
-                src_ref=sb.at[to_y, to // 2, to % 2], dst_ref=sr.at[me],
-                send_sem=send_sem.at[3], recv_sem=recv_sem.at[3],
-                device_id={"turn": to * 4 + to_y}, device_id_type=MESH,
-            ).start()
-            return 0
-
-        lax.fori_loop(1 if c == 0 else 0, 32, send_beams, 0)
-    sr[me] = sb[y, xz // 2, xz % 2]
-
-    pltpu.make_async_copy(sr.at[pl.ds(0, 127)], sr.at[pl.ds(0, 127)], recv_sem.at[3]).wait()
-
-    def east_west(at, _):
+    def east_west(zl, from_y):
+        at = zl * 4 + from_y
         ns = [[None] * 4, [None] * 4]
         for c in range(4):
             one = sr[c * GROUP + at].astype(F32)
@@ -311,17 +338,20 @@
         for high in range(2):
             for r in range(2):
                 first, second = swap(chirped[2 * high][r], chirped[2 * high + 1][r], 0, 4)
-                vs[r, 0, at, high] = first
-                vs[r, 1, at, high] = second
-        return 0
-
-    lax.fori_loop(0, GROUP, east_west, 0)
+                vs[r, 0, at, 8 * high : 8 * high + 8] = first
+                vs[r, 1, at, 8 * high : 8 * high + 8] = second
+        return from_y
+
+    for c in range(4):
+        count = 32 if c else 31
+        pltpu.make_async_copy(sr.at[pl.ds(0, count)], sr.at[pl.ds(0, count)], beam_sem.at[c]).wait()
+        lax.fori_loop(0, 4, east_west, (y + 4 - c) % 4)
 
     for r in range(2):
         for h in range(2):
-            turned = exchange(vs[r, h], 4, 8).reshape(2, 8, 16, 128).astype(BF16)
-            ys[2 * h, :, :, r * 128 : (r + 1) * 128] = turned[0]
-            ys[2 * h + 1, :, :, r * 128 : (r + 1) * 128] = turned[1]
+            items = gather([vs[r, h, i] for i in range(GROUP)], 8)
+            for k in range(GROUP):
+                ys[2 * h + k // 8, k % 8, :, r * 128 : (r + 1) * 128] = items[k].astype(BF16)
 
     def synthesise(f):
         z = jnp.dot(ys[f].reshape(128, 256), iv[...], preferred_element_type=F32).reshape(8, 16, 512)
@@ -340,41 +370,47 @@
             if f < 3:
                 wb[f, :, n * SHORT : (n + 1) * SHORT] = outs[n].astype(BF16)
 
+    future = [
+        pltpu.make_async_remote_copy(
+            src_ref=wb.at[f], dst_ref=wr.at[f], send_sem=fut_sem.at[0, f], recv_sem=fut_sem.at[1, f],
+            device_id={"tm": before}, device_id_type=MESH,
+        )
+        for f in range(3)
+    ]
     for f in range(3):
         synthesise(f)
-    future = pltpu.make_async_remote_copy(
-        src_ref=wb, dst_ref=wr, send_sem=send_sem.at[4], recv_sem=recv_sem.at[4],
-        device_id={"tm": before}, device_id_type=MESH,
-    )
-    future.start()
+        future[f].start()
     synthesise(3)
 
     last = jnp.where(tm < 3, 1.0, 0.0).astype(F32)
 
-    def wave_of(at):
-        if at > 3:
-            return wr[at - 4].astype(F32) * last
-        return wf[at]
-
-    stores = []
-    for f in range(FRAMES):
-        if f == 1:
-            future.wait_recv()
-        total = wv[3:4, :] * wave_of(f)
-        for p in range(1, TAPS):
-            total = total + wv[3 - p : 4 - p, :] * wave_of(f + p)
-        ov[:, f * NFFT : (f + 1) * NFFT] = total
+    def store_frame(f):
         store = pltpu.make_async_copy(
             ov.at[:, pl.ds(f * NFFT, NFFT)], out.at[:, pl.ds(f * NFFT, NFFT)], out_sem.at[f]
         )
         store.start()
-        stores.append(store)
-
-    history.wait_send()
-    future.wait_send()
-    pltpu.make_async_copy(gr.at[pl.ds(0, QUADS - 1)], gr.at[pl.ds(0, QUADS - 1)], send_sem.at[1]).wait()
-    pltpu.make_async_copy(ra.at[pl.ds(0, GROUP - 1)], ra.at[pl.ds(0, GROUP - 1)], send_sem.at[2]).wait()
-    pltpu.make_async_copy(sr.at[pl.ds(0, 127)], sr.at[pl.ds(0, 127)], send_sem.at[3]).wait()
+        return store
+
+    for f in range(FRAMES):
+        total = wv[3:4, :] * wf[f]
+        for p in range(1, FRAMES - f):
+            total = total + wv[3 - p : 4 - p, :] * wf[f + p]
+        ov[:, f * NFFT : (f + 1) * NFFT] = total
+    stores = [store_frame(0)]
+    for f in range(1, FRAMES):
+        future[f - 1].wait_recv()
+        total = ov[:, f * NFFT : (f + 1) * NFFT]
+        for p in range(FRAMES - f, TAPS):
+            total = total + (wv[3 - p : 4 - p, :] * last) * wr[f + p - 4].astype(F32)
+        ov[:, f * NFFT : (f + 1) * NFFT] = total
+        stores.append(store_frame(f))
+
+    for copy in history + future:
+        copy.wait_send()
+    pltpu.make_async_copy(gr.at[pl.ds(0, QUADS - 1)], gr.at[pl.ds(0, QUADS - 1)], send_sem.at[0]).wait()
+    for f in range(FRAMES):
+        pltpu.make_async_copy(ra.at[f, pl.ds(0, GROUP - 1)], ra.at[f, pl.ds(0, GROUP - 1)], send_sem.at[1]).wait()
+    pltpu.make_async_copy(sr.at[pl.ds(0, 127)], sr.at[pl.ds(0, 127)], send_sem.at[2]).wait()
     for store in stores:
         store.wait()
 
@@ -389,7 +425,7 @@
         out_specs=anywhere,
         scratch_shapes=[
             vmem((16, FRAMES * NFFT), BF16),
-            vmem((16, 3 * NFFT), BF16),
+            vmem((3, 16, NFFT), BF16),
             vmem((2, 8, 2048), F32),
             vmem((TAPS, NFFT), F32),
             vmem((8, 2, SHORT), F32),
@@ -400,14 +436,15 @@
             vmem((16, 2048), BF16),
             vmem((QUADS, 16, FEEDS), BF16),
             vmem((2, 8, 2, 8, 128), F32),
-            vmem((512, 512), BF16),
-            vmem((256, 512), BF16),
-            vmem((GROUP, 16, 512), BF16),
+            vmem((FRAMES, 128, 512), BF16),
+            vmem((FRAMES, GROUP, 16, 128), BF16),
+            vmem((FRAMES, GROUP, 16, 128), BF16),
+            vmem((256, 512), F32),
             vmem((256, 512), BF16),
             vmem((4, 16, 2, 8, 128), BF16),
             vmem((128, 8, 128), BF16),
             vmem((GROUP, 2, 4, 8, 128), F32),
-            vmem((2, 2, GROUP, 2, 8, 128), F32),
+            vmem((2, 2, GROUP, 16, 128), F32),
             vmem((FRAMES, 8, 16, 256), BF16),
             vmem((FRAMES, 16, NFFT), F32),
             vmem((3, 16, NFFT), BF16),
@@ -415,11 +452,15 @@
             vmem((16, FRAMES * NFFT), F32),
             pltpu.SemaphoreType.DMA((8,)),
             pltpu.SemaphoreType.DMA((FRAMES,)),
-            pltpu.SemaphoreType.DMA((5,)),
-            pltpu.SemaphoreType.DMA((5,)),
+            pltpu.SemaphoreType.DMA((3,)),
+            pltpu.SemaphoreType.DMA((1,)),
+            pltpu.SemaphoreType.DMA((2, 3)),
+            pltpu.SemaphoreType.DMA((FRAMES,)),
+            pltpu.SemaphoreType.DMA((4,)),
+            pltpu.SemaphoreType.DMA((2, 3)),
         ],
         compiler_params=pltpu.CompilerParams(
-            collective_id=0, has_side_effects=True, vmem_limit_bytes=40 * 1024 * 1024
+            collective_id=0, has_side_effects=True, vmem_limit_bytes=60 * 1024 * 1024
         ),
         cost_estimate=pl.CostEstimate(flops=500_000_000, bytes_accessed=3_000_000, transcendentals=0),
     )(

time: 61.4 us -> 54.6 us (0.89)
  local copies, waits for them, and re-layouts: 8.1 us -> 2.18 us
  Pallas kernels: 52.9 us -> 52.2 us
    unnamed x18 -> x0, local copies, waits for them, and re-layouts: 6.97 us -> none
    reshape x1, local copies, waits for them, and re-layouts: 0.31 us -> 1.35 us  [body(): ordered = rows.reshape(4, 2, 2, FRAMES * NFFT).transpose(1, 0, 2, 3)]
    pallas_call x1, Pallas kernels: 52.9 us -> 52.2 us  [body(): pl.pallas_call(kernel, out_shape=jax.ShapeDtypeStruct((16, FRAMES * NFFT)...]
where the time goes in v1:
time: 54.6 us; the launch traced here: 54.4 us
  Pallas kernels  52.2 us (96%)
  local copies, waits for them, and re-layouts  2.18 us (4%)
    pallas_call x1, Pallas kernels, body(): pl.pallas_call(kernel, out_shape=jax.ShapeDtypeStruct((16, FRAMES * NFFT)...  52.2 us
    reshape x1, local copies, waits for them, and re-layouts, body(): ordered = rows.reshape(4, 2, 2, FRAMES * NFFT).transpose(1, 0, 2, 3)  1.35 us

profile of v1, /device:TPU:1, one launch (start us, length us, event | category | flops | bytes accessed | tf_op | source)
XLA Modules:
  0.0 54.4 jit_solution(590802045841889470)
XLA Ops:
  0.0 52.2 %shard_map.91 = f32[16,8192]{1,0:T(8,128)} custom-call(bf16[16,8192]{1,0:T(8,128)(2,1)} %volt.1, f32[2,8,2048]{2,1,0:T(8,128)} %bitcast.4, f32[8]{0:T(128)} %disp.1, f32[4,2048]{1,0:T(4,128)} %constant.12.clone.window, f32[8,2,256]{2,1,0:T(2,128)} %constant.13.clone.twid, bf16[256,512]{1,0:T(8,128)(2,1)} %constant.14.clone.fwd, ...), custom_call_target="tpu_custom_call" | custom-call | flops 500000000 | bytes 3000000 | tf_op jit(solution)/shard_map/pallas_call | solution.py:421
  52.3 1.3 %reshape.6 = f32[4,2,2,8192]{3,2,1,0:T(2,128)S(1)} reshape(f32[16,8192]{1,0:T(8,128)} %shard_map.91) | data formatting | bytes 1048576 | tf_op jit(solution)/shard_map/reshape | solution.py:470
  53.6 0.8 %copy.10 = f32[2,4,2,8192]{3,2,1,0:T(2,128)} copy(f32[2,4,2,8192]{3,2,0,1:T(2,128)S(1)} %bitcast.3) | data formatting | bytes 1048576 | tf_op jit(solution)/shard_map/transpose | solution.py:470

commit v2 on v1

--- a/solution.py
+++ b/solution.py
@@ -131,27 +131,28 @@
 
 def kernel(
     volt, gain, disp, window, twid, fwd, inv, beam, space, out,
-    xv, xh, gv, wv, tv, fv, iv, bv, sv, gb, gr, gt, zs, ab, ra, xs, xb, sb, sr, ct, vs, ys, wf, wb, wr, ov,
+    xv, xh, gv, wv, tv, fv, iv, bv, sv, gb, gr, gt, zs, al, rl, ab, ra, xs, xb, sb, sr, ct, vs, ys, wf, wb, wr, ov,
     load_sem, out_sem, send_sem, recv_sem, hist_sem, chan_sem, beam_sem, fut_sem,
 ):
     me, tm = lax.axis_index("turn"), lax.axis_index("tm")
-    base, g = (me // GROUP) * GROUP, me % GROUP
-    xz, y = me // 4, me % 4
-    after, before = (tm + 1) % 4, (tm + 3) % 4
+    mine, g = lax.div(me, GROUP), lax.rem(me, GROUP)
+    base = mine * GROUP
+    xz, y = lax.div(me, 4), lax.rem(me, 4)
+    after, before = lax.rem(tm + 1, 4), lax.rem(tm + 3, 4)
 
     barrier = pltpu.get_barrier_semaphore()
 
     def greet_group(i, _):
-        pl.semaphore_signal(barrier, inc=1, device_id={"turn": base + (g + i) % GROUP}, device_id_type=MESH)
+        pl.semaphore_signal(barrier, inc=1, device_id={"turn": base + lax.rem(g + i, GROUP)}, device_id_type=MESH)
         return 0
 
     def greet_quads(i, _):
-        pl.semaphore_signal(barrier, inc=1, device_id={"turn": (me + GROUP * i) % 128}, device_id_type=MESH)
+        pl.semaphore_signal(barrier, inc=1, device_id={"turn": lax.rem(me + GROUP * i, 128)}, device_id_type=MESH)
         return 0
 
+    lax.fori_loop(1, QUADS, greet_quads, 0)
     for other in (after, before):
         pl.semaphore_signal(barrier, inc=1, device_id={"tm": other}, device_id_type=MESH)
-    lax.fori_loop(1, QUADS, greet_quads, 0)
     lax.fori_loop(1, GROUP, greet_group, 0)
 
     loads = [
@@ -166,6 +167,19 @@
     loads[1].wait()
     gb[...] = gv[...].reshape(16, 2048).astype(BF16)
     pl.semaphore_wait(barrier, 2 + QUADS - 1 + GROUP - 1)
+
+
+    def send_gain(i, _):
+        q = lax.rem(mine + i, QUADS)
+        pltpu.make_async_remote_copy(
+            src_ref=gb.at[:, pl.ds(pl.multiple_of(q * FEEDS, FEEDS), FEEDS)], dst_ref=gr.at[mine],
+            send_sem=send_sem.at[0], recv_sem=recv_sem.at[0],
+            device_id={"turn": q * GROUP + g}, device_id_type=MESH,
+        ).start()
+        return 0
+
+    lax.fori_loop(1, QUADS, send_gain, 0)
+    gr[mine] = gb[:, pl.ds(pl.multiple_of(mine * FEEDS, FEEDS), FEEDS)]
 
     history = [
         pltpu.make_async_remote_copy(
@@ -202,49 +216,38 @@
                 zr, zi = re * c - im * s, re * s + im * c
             else:
                 zr, zi = re * c + im * s, re * s - im * c
-            rows = pl.ds(pl.multiple_of((k1 + g) % 8 * 16, 16), 16)
+            rows = pl.ds(pl.multiple_of(lax.rem(k1 + g, 8) * 16, 16), 16)
             zs[f, rows, 0:SHORT] = zr.astype(BF16)
             zs[f, rows, SHORT : 2 * SHORT] = zi.astype(BF16)
 
     contract = (((1,), (1,)), ((), ()))
 
-    def exchange_channels(f):
+    def transform(f):
         channels = lax.dot_general(fv[...], zs[f], contract, preferred_element_type=F32)
-        ab[f] = channels.reshape(GROUP, 16, 128).astype(BF16)
-
+        return channels.reshape(GROUP, 16, 128).astype(BF16)
+
+    def exchange_channels(part, source, target):
         def send_channels(i, _):
-            to = (g + i) % GROUP
+            to = lax.rem(g + i, GROUP)
             pltpu.make_async_remote_copy(
-                src_ref=ab.at[f, to], dst_ref=ra.at[f, g],
-                send_sem=send_sem.at[1], recv_sem=chan_sem.at[f],
+                src_ref=source.at[to], dst_ref=target.at[g],
+                send_sem=chan_sem.at[0, part], recv_sem=chan_sem.at[1, part],
                 device_id={"turn": base + to}, device_id_type=MESH,
             ).start()
             return 0
 
         lax.fori_loop(1, GROUP, send_channels, 0)
-        ra[f, g] = ab[f, g]
+        target[g] = source[g]
 
     channelize(3)
-    exchange_channels(3)
-
-    mine = me // GROUP
-
-    def send_gain(i, _):
-        q = (mine + i) % QUADS
-        pltpu.make_async_remote_copy(
-            src_ref=gb.at[:, pl.ds(pl.multiple_of(q * FEEDS, FEEDS), FEEDS)], dst_ref=gr.at[mine],
-            send_sem=send_sem.at[0], recv_sem=recv_sem.at[0],
-            device_id={"turn": q * GROUP + g}, device_id_type=MESH,
-        ).start()
-        return 0
-
-    lax.fori_loop(1, QUADS, send_gain, 0)
-    gr[mine] = gb[:, pl.ds(pl.multiple_of(mine * FEEDS, FEEDS), FEEDS)]
+    al[...] = transform(3)
+    exchange_channels(0, al, rl)
 
     for f in (2, 1, 0):
         history[f].wait_recv()
         channelize(f)
-        exchange_channels(f)
+        ab[:, f] = transform(f)
+    exchange_channels(1, ab, ra)
 
     pltpu.make_async_copy(gr.at[pl.ds(0, QUADS - 1)], gr.at[pl.ds(0, QUADS - 1)], recv_sem.at[0]).wait()
     for half in range(2):
@@ -259,52 +262,60 @@
 
     loads[6].wait()
     loads[5].wait()
+    turned_rows = [lax.rem(g + i, 16) * 8 for i in range(16)]
     for f in (3, 2, 1, 0):
-        pltpu.make_async_copy(ra.at[f, pl.ds(0, GROUP - 1)], ra.at[f, pl.ds(0, GROUP - 1)], chan_sem.at[f]).wait()
+        if f >= 2:
+            arrived = rl if f == 3 else ra
+            rest = arrived.at[pl.ds(0, GROUP - 1)]
+            pltpu.make_async_copy(rest, rest, chan_sem.at[1, 3 - f]).wait()
         for half in range(2):
-            items = gather([ra[f, half * 8 + i].astype(F32) for i in range(8)], 16)
+            items = [half * 8 + i for i in range(8)]
+            items = [(rl[i] if f == 3 else ra[i, f]).astype(F32) for i in items]
+            items = gather(items, 16)
             for k1 in range(8):
                 re, im = items[k1][:8], items[k1][8:]
                 gre, gim = gt[half, k1, 0], gt[half, k1, 1]
-                rows = pl.ds(pl.multiple_of((f // 2) * 128 + ((f % 2) * 8 + k1 + g) % 16 * 8, 8), 8)
+                rows = pl.ds(pl.multiple_of((f // 2) * 128 + turned_rows[(f % 2) * 8 + k1], 8), 8)
                 xs[rows, half * 128 : (half + 1) * 128] = gre * re - gim * im
                 xs[rows, FEEDS + half * 128 : FEEDS + (half + 1) * 128] = gre * im + gim * re
     xb[...] = xs[...].astype(BF16)
 
     row3 = lax.broadcasted_iota(jnp.int32, (16, 8, 128), 1)
-    xh_me, z_me = me // 64, xz % 16
+    x_me, z_me = lax.div(me, 64), lax.rem(xz, 16)
+    x_at, y_at = [x_me * 16, 16 - x_me * 16], [lax.rem(y + c, 4) for c in range(4)]
     for pair in range(2):
         for c in (2 * pair, 2 * pair + 1):
-            to_y = (y + c) % 4
+            to_y = y_at[c]
             both = lax.dot_general(
                 bv[pl.ds(pl.multiple_of(to_y * 128, 128), 128), :], xb[...], contract, preferred_element_type=F32
             )
             low, high = both[:, :128].reshape(16, 8, 128), both[:, 128:].reshape(16, 8, 128)
-            sb[to_y, :, 0] = jnp.where(row3 < 4, low, pltpu.roll(high, 4, 1)).astype(BF16)
-            sb[to_y, :, 1] = jnp.where(row3 < 4, pltpu.roll(low, 4, 1), high).astype(BF16)
-
-        def send_beams(c, x_by, z_by):
-            to_y = (y + c) % 4
-            to = ((xh_me + x_by) % 2) * 16 + (z_me + z_by) % 16
+            even = jnp.where(row3 < 4, low, pltpu.roll(high, 4, 1))
+            odd = jnp.where(row3 < 4, pltpu.roll(low, 4, 1), high)
+            sb[to_y] = jnp.stack([even, odd], axis=1).reshape(32, 8, 128).astype(BF16)
+
+        def send_beams(c, x_by, z_to):
+            to_y = y_at[c]
+            to = x_at[x_by] + z_to
             pltpu.make_async_remote_copy(
-                src_ref=sb.at[to_y, to // 2, to % 2], dst_ref=sr.at[me],
+                src_ref=sb.at[to_y, to], dst_ref=sr.at[me],
                 send_sem=send_sem.at[2], recv_sem=beam_sem.at[c],
                 device_id={"turn": to * 4 + to_y}, device_id_type=MESH,
             ).start()
 
         def send_far(i, _):
-            z_by = 8 + (1 - 2 * (i % 2)) * ((i + 1) // 2)
+            z_to = lax.rem(z_me + 8 + (1 - 2 * lax.rem(i, 2)) * lax.div(i + 1, 2), 16)
             for c in (2 * pair, 2 * pair + 1):
                 for x_by in range(2):
-                    send_beams(c, x_by, z_by)
+                    send_beams(c, x_by, z_to)
             return 0
 
         lax.fori_loop(0, 15, send_far, 0)
         for c in (2 * pair, 2 * pair + 1):
             for x_by in range(2):
                 if c + x_by > 0:
-                    send_beams(c, x_by, 0)
-    sr[me] = sb[y, xz // 2, xz % 2]
+                    send_beams(c, x_by, z_me)
+    sr[me] = sb[y, xz]
 
     loads[7].wait()
     row = lax.broadcasted_iota(jnp.int32, (8, 128), 0)
@@ -335,17 +346,19 @@
             re, im = beams[e]
             c, s = ct[at, 0, e], ct[at, 1, e]
             chirped.append((re * c - im * s, re * s + im * c))
-        for high in range(2):
-            for r in range(2):
-                first, second = swap(chirped[2 * high][r], chirped[2 * high + 1][r], 0, 4)
-                vs[r, 0, at, 8 * high : 8 * high + 8] = first
-                vs[r, 1, at, 8 * high : 8 * high + 8] = second
+        for r in range(2):
+            even = swap(chirped[0][r], chirped[2][r], 0, 4)
+            odd = swap(chirped[1][r], chirped[3][r], 0, 4)
+            for h in range(2):
+                first, second = swap(even[h], odd[h], 0, 2)
+                vs[r, h, at, :8] = first
+                vs[r, h, at, 8:] = second
         return from_y
 
     for c in range(4):
         count = 32 if c else 31
         pltpu.make_async_copy(sr.at[pl.ds(0, count)], sr.at[pl.ds(0, count)], beam_sem.at[c]).wait()
-        lax.fori_loop(0, 4, east_west, (y + 4 - c) % 4)
+        lax.fori_loop(0, 4, east_west, lax.rem(y + 4 - c, 4))
 
     for r in range(2):
         for h in range(2):
@@ -408,8 +421,9 @@
     for copy in history + future:
         copy.wait_send()
     pltpu.make_async_copy(gr.at[pl.ds(0, QUADS - 1)], gr.at[pl.ds(0, QUADS - 1)], send_sem.at[0]).wait()
-    for f in range(FRAMES):
-        pltpu.make_async_copy(ra.at[f, pl.ds(0, GROUP - 1)], ra.at[f, pl.ds(0, GROUP - 1)], send_sem.at[1]).wait()
+    for part, target in ((0, rl), (1, ra)):
+        rest = target.at[pl.ds(0, GROUP - 1)]
+        pltpu.make_async_copy(rest, rest, chan_sem.at[0, part]).wait()
     pltpu.make_async_copy(sr.at[pl.ds(0, 127)], sr.at[pl.ds(0, 127)], send_sem.at[2]).wait()
     for store in stores:
         store.wait()
@@ -437,11 +451,13 @@
             vmem((QUADS, 16, FEEDS), BF16),
             vmem((2, 8, 2, 8, 128), F32),
             vmem((FRAMES, 128, 512), BF16),
-            vmem((FRAMES, GROUP, 16, 128), BF16),
-            vmem((FRAMES, GROUP, 16, 128), BF16),
+            vmem((GROUP, 16, 128), BF16),
+            vmem((GROUP, 16, 128), BF16),
+            vmem((GROUP, 3, 16, 128), BF16),
+            vmem((GROUP, 3, 16, 128), BF16),
             vmem((256, 512), F32),
             vmem((256, 512), BF16),
-            vmem((4, 16, 2, 8, 128), BF16),
+            vmem((4, 32, 8, 128), BF16),
             vmem((128, 8, 128), BF16),
             vmem((GROUP, 2, 4, 8, 128), F32),
             vmem((2, 2, GROUP, 16, 128), F32),
@@ -455,7 +471,7 @@
             pltpu.SemaphoreType.DMA((3,)),
             pltpu.SemaphoreType.DMA((1,)),
             pltpu.SemaphoreType.DMA((2, 3)),
-            pltpu.SemaphoreType.DMA((FRAMES,)),
+            pltpu.SemaphoreType.DMA((2, 2)),
             pltpu.SemaphoreType.DMA((4,)),
             pltpu.SemaphoreType.DMA((2, 3)),
         ],
@@ -467,8 +483,7 @@
         voltages, gains.transpose(0, 2, 1), dispersion,
         window_rows(), twiddle_rows(), forward_table(), inverse_table(), beam_table(), spacing_rows(),
     )
-    ordered = rows.reshape(4, 2, 2, FRAMES * NFFT).transpose(1, 0, 2, 3)
-    return ordered.reshape(8, 2, FRAMES * NFFT)
+    return rows.reshape(8, 2, FRAMES * NFFT)
 
 
 def solution(mesh):

time: 54.6 us -> 53.4 us (0.978)
  Pallas kernels: 52.2 us -> 51.1 us
    pallas_call x1, Pallas kernels: 52.2 us -> 51.1 us  [body(): pl.pallas_call(kernel, out_shape=jax.ShapeDtypeStruct((16, FRAMES * NFFT)...]
    transpose x1 -> x0, local copies, waits for them, and re-layouts: 0.83 us -> none  [body(): ordered = rows.reshape(4, 2, 2, FRAMES * NFFT).transpose(1, 0, 2, 3)]
    reshape x1, local copies, waits for them, and re-layouts: 1.35 us -> 2.14 us  [body(): return rows.reshape(8, 2, FRAMES * NFFT)]
where the time goes in v2:
time: 53.4 us; the launch traced here: 53.2 us
  Pallas kernels  51.1 us (96%)
  local copies, waits for them, and re-layouts  2.14 us (4%)
    pallas_call x1, Pallas kernels, body(): pl.pallas_call(kernel, out_shape=jax.ShapeDtypeStruct((16, FRAMES * NFFT)...  51.1 us
    reshape x1, local copies, waits for them, and re-layouts, body(): return rows.reshape(8, 2, FRAMES * NFFT)  2.14 us

profile of v2, /device:TPU:1, one launch (start us, length us, event | category | flops | bytes accessed | tf_op | source)
XLA Modules:
  0.0 53.2 jit_solution(16152112329423319012)
XLA Ops:
  0.0 51.1 %shard_map.91 = f32[16,8192]{1,0:T(8,128)} custom-call(bf16[16,8192]{1,0:T(8,128)(2,1)} %volt.1, f32[2,8,2048]{2,1,0:T(8,128)} %bitcast.1, f32[8]{0:T(128)} %disp.1, f32[4,2048]{1,0:T(4,128)} %constant.12.clone.window, f32[8,2,256]{2,1,0:T(2,128)} %constant.13.clone.twid, bf16[256,512]{1,0:T(8,128)(2,1)} %constant.14.clone.fwd, ...), custom_call_target="tpu_custom_call" | custom-call | flops 500000000 | bytes 3000000 | tf_op jit(solution)/shard_map/pallas_call | solution.py:435
  51.1 2.1 %reshape.3 = f32[8,2,8192]{2,1,0:T(2,128)} reshape(f32[16,8192]{1,0:T(8,128)} %shard_map.91) | data formatting | bytes 1048576 | tf_op jit(solution)/shard_map/reshape | solution.py:486

commit v3 on v2

--- a/solution.py
+++ b/solution.py
@@ -125,13 +125,9 @@
     )
 
 
-def turned_phase(turns):
-    return jnp.cos(turns), jnp.sin(turns)
-
-
 def kernel(
     volt, gain, disp, window, twid, fwd, inv, beam, space, out,
-    xv, xh, gv, wv, tv, fv, iv, bv, sv, gb, gr, gt, zs, al, rl, ab, ra, xs, xb, sb, sr, ct, vs, ys, wf, wb, wr, ov,
+    xv, xh, gv, wv, tv, fv, iv, bv, sv, gb, gr, gt, zs, al, rl, ab, ra, xs, xb, sb, sr, ct, vs, ys, wf, wb, wr, pv, ov,
     load_sem, out_sem, send_sem, recv_sem, hist_sem, chan_sem, beam_sem, fut_sem,
 ):
     me, tm = lax.axis_index("turn"), lax.axis_index("tm")
@@ -283,38 +279,37 @@
     row3 = lax.broadcasted_iota(jnp.int32, (16, 8, 128), 1)
     x_me, z_me = lax.div(me, 64), lax.rem(xz, 16)
     x_at, y_at = [x_me * 16, 16 - x_me * 16], [lax.rem(y + c, 4) for c in range(4)]
-    for pair in range(2):
-        for c in (2 * pair, 2 * pair + 1):
-            to_y = y_at[c]
-            both = lax.dot_general(
-                bv[pl.ds(pl.multiple_of(to_y * 128, 128), 128), :], xb[...], contract, preferred_element_type=F32
-            )
-            low, high = both[:, :128].reshape(16, 8, 128), both[:, 128:].reshape(16, 8, 128)
-            even = jnp.where(row3 < 4, low, pltpu.roll(high, 4, 1))
-            odd = jnp.where(row3 < 4, pltpu.roll(low, 4, 1), high)
-            sb[to_y] = jnp.stack([even, odd], axis=1).reshape(32, 8, 128).astype(BF16)
-
-        def send_beams(c, x_by, z_to):
-            to_y = y_at[c]
-            to = x_at[x_by] + z_to
-            pltpu.make_async_remote_copy(
-                src_ref=sb.at[to_y, to], dst_ref=sr.at[me],
-                send_sem=send_sem.at[2], recv_sem=beam_sem.at[c],
-                device_id={"turn": to * 4 + to_y}, device_id_type=MESH,
-            ).start()
-
-        def send_far(i, _):
-            z_to = lax.rem(z_me + 8 + (1 - 2 * lax.rem(i, 2)) * lax.div(i + 1, 2), 16)
-            for c in (2 * pair, 2 * pair + 1):
-                for x_by in range(2):
-                    send_beams(c, x_by, z_to)
-            return 0
-
-        lax.fori_loop(0, 15, send_far, 0)
-        for c in (2 * pair, 2 * pair + 1):
+    for c in range(4):
+        to_y = y_at[c]
+        both = lax.dot_general(
+            bv[pl.ds(pl.multiple_of(to_y * 128, 128), 128), :], xb[...], contract, preferred_element_type=F32
+        )
+        low, high = both[:, :128].reshape(16, 8, 128), both[:, 128:].reshape(16, 8, 128)
+        even = jnp.where(row3 < 4, low, pltpu.roll(high, 4, 1))
+        odd = jnp.where(row3 < 4, pltpu.roll(low, 4, 1), high)
+        sb[to_y] = jnp.stack([even, odd], axis=1).reshape(32, 8, 128).astype(BF16)
+
+    def send_beams(c, x_by, z_to):
+        to_y = y_at[c]
+        to = x_at[x_by] + z_to
+        pltpu.make_async_remote_copy(
+            src_ref=sb.at[to_y, to], dst_ref=sr.at[me],
+            send_sem=send_sem.at[2], recv_sem=beam_sem.at[c],
+            device_id={"turn": to * 4 + to_y}, device_id_type=MESH,
+        ).start()
+
+    def send_far(i, _):
+        z_to = lax.rem(z_me + 8 + (1 - 2 * lax.rem(i, 2)) * lax.div(i + 1, 2), 16)
+        for c in range(4):
             for x_by in range(2):
-                if c + x_by > 0:
-                    send_beams(c, x_by, z_me)
+                send_beams(c, x_by, z_to)
+        return 0
+
+    lax.fori_loop(0, 15, send_far, 0)
+    for c in range(4):
+        for x_by in range(2):
+            if c + x_by > 0:
+                send_beams(c, x_by, z_me)
     sr[me] = sb[y, xz]
 
     loads[7].wait()
@@ -323,7 +318,7 @@
     def phases(at, _):
         for e in range(4):
             scale = jnp.where((row & 2) == 0, disp[e], disp[4 + e])
-            c, s = turned_phase(scale * sv[pl.ds(at, 1), :])
+            c, s = jnp.cos(scale * sv[pl.ds(at, 1), :]), jnp.sin(scale * sv[pl.ds(at, 1), :])
             ct[at, 0, e] = 0.5 * c
             ct[at, 1, e] = 0.5 * s
         return 0
@@ -397,9 +392,13 @@
 
     last = jnp.where(tm < 3, 1.0, 0.0).astype(F32)
 
+    def place(f, total):
+        for b in range(8):
+            ov[b, :, f * NFFT : (f + 1) * NFFT] = total[2 * b : 2 * b + 2]
+
     def store_frame(f):
         store = pltpu.make_async_copy(
-            ov.at[:, pl.ds(f * NFFT, NFFT)], out.at[:, pl.ds(f * NFFT, NFFT)], out_sem.at[f]
+            ov.at[:, :, pl.ds(f * NFFT, NFFT)], out.at[:, :, pl.ds(f * NFFT, NFFT)], out_sem.at[f]
         )
         store.start()
         return store
@@ -408,14 +407,17 @@
         total = wv[3:4, :] * wf[f]
         for p in range(1, FRAMES - f):
             total = total + wv[3 - p : 4 - p, :] * wf[f + p]
-        ov[:, f * NFFT : (f + 1) * NFFT] = total
+        if f == 0:
+            place(0, total)
+        else:
+            pv[f - 1] = total
     stores = [store_frame(0)]
     for f in range(1, FRAMES):
         future[f - 1].wait_recv()
-        total = ov[:, f * NFFT : (f + 1) * NFFT]
+        total = pv[f - 1]
         for p in range(FRAMES - f, TAPS):
             total = total + (wv[3 - p : 4 - p, :] * last) * wr[f + p - 4].astype(F32)
-        ov[:, f * NFFT : (f + 1) * NFFT] = total
+        place(f, total)
         stores.append(store_frame(f))
 
     for copy in history + future:
@@ -432,9 +434,9 @@
 def body(voltages, gains, dispersion):
     anywhere = pl.BlockSpec(memory_space=pl.ANY)
     vmem = pltpu.VMEM
-    rows = pl.pallas_call(
+    return pl.pallas_call(
         kernel,
-        out_shape=jax.ShapeDtypeStruct((16, FRAMES * NFFT), F32),
+        out_shape=jax.ShapeDtypeStruct((8, 2, FRAMES * NFFT), F32),
         in_specs=[anywhere, anywhere, pl.BlockSpec(memory_space=pltpu.SMEM)] + [anywhere] * 6,
         out_specs=anywhere,
         scratch_shapes=[
@@ -465,7 +467,8 @@
             vmem((FRAMES, 16, NFFT), F32),
             vmem((3, 16, NFFT), BF16),
             vmem((3, 16, NFFT), BF16),
-            vmem((16, FRAMES * NFFT), F32),
+            vmem((3, 16, NFFT), F32),
+            vmem((8, 2, FRAMES * NFFT), F32),
             pltpu.SemaphoreType.DMA((8,)),
             pltpu.SemaphoreType.DMA((FRAMES,)),
             pltpu.SemaphoreType.DMA((3,)),
@@ -483,7 +486,6 @@
         voltages, gains.transpose(0, 2, 1), dispersion,
         window_rows(), twiddle_rows(), forward_table(), inverse_table(), beam_table(), spacing_rows(),
     )
-    return rows.reshape(8, 2, FRAMES * NFFT)
 
 
 def solution(mesh):

time: 53.4 us -> 52.7 us (0.987)
    reshape x1 -> x0, local copies, waits for them, and re-layouts: 2.14 us -> none  [body(): return rows.reshape(8, 2, FRAMES * NFFT)]
    unnamed x0 -> x1, local copies, waits for them, and re-layouts: none -> 1.87 us
where the time goes in v3:
time: 52.7 us; the launch traced here: 52.5 us
  Pallas kernels  50.6 us (96%)
  local copies, waits for them, and re-layouts  1.87 us (4%)
    pallas_call x1, Pallas kernels, body(): pl.pallas_call(kernel, out_shape=jax.ShapeDtypeStruct((8, 2, FRAMES * NFF...  50.6 us
    unnamed x1, local copies, waits for them, and re-layouts  1.87 us

profile of v3, /device:TPU:1, one launch (start us, length us, event | category | flops | bytes accessed | tf_op | source)
XLA Modules:
  0.0 52.5 jit_solution(3517651540143831853)
XLA Ops:
  0.0 50.6 %shard_map.91 = f32[8,2,8192]{2,1,0:T(2,128)} custom-call(bf16[16,8192]{1,0:T(8,128)(2,1)} %volt.1, f32[2,8,2048]{2,1,0:T(8,128)} %bitcast.1, f32[8]{0:T(128)} %disp.1, f32[4,2048]{1,0:T(4,128)} %constant.12.clone.window, f32[8,2,256]{2,1,0:T(2,128)} %constant.13.clone.twid, bf16[256,512]{1,0:T(8,128)(2,1)} %constant.14.clone.fwd, ...), custom_call_target="tpu_custom_call" | custom-call | flops 500000000 | bytes 3000000 | tf_op jit(solution)/shard_map/pallas_call | solution.py:437
  50.7 1.9 %copy.11 = f32[8,2,8192]{2,1,0:T(2,128)} copy(f32[8,2,8192]{2,1,0:T(2,128)} %shard_map.91) | data formatting | bytes 1048576
